TPU v7x, 512 devices: a whole 4x8x8 slice. The times are simulated.
512 devices in a mesh: lon: 32 (over z_lo, y, core), lat: 16 (over z_hi, x).
Axes of the slice: x: 4, y: 8, z: 8 (z_hi: 4, z_lo: 2; z = z_hi * 2 + z_lo), core: 2. Of those that a mesh axis runs over, the one named last changes fastest.
Arguments:
- tokens: bfloat16 [384, 128, 1024], P('lon', 'lat'), may hold values from -6 to 6
- query_local: bfloat16 [384, 128, 1024], P('lon', 'lat'), may hold values from -21 to 21, as said below
- key_local: bfloat16 [384, 128, 1024], P('lon', 'lat'), may hold values from -21 to 21, as said below
- value_local: bfloat16 [384, 128, 1024], P('lon', 'lat'), may hold values from -6 to 6
- position_bias: float32 [16, 13, 13], replicated, may hold values from -4 to 4
- output_weight: bfloat16 [1024, 1024], P('lat'), may hold values from -0.1875 to 0.1875
- norm_gain: float32 [1024], replicated, may hold values from 0.1 to 1.9
- global_weight: bfloat16 [1024, 3072], P('lat'), may hold values from -1 to 1
Outputs:
- hidden: bfloat16 [384, 128, 1024], P('lon', 'lat')
- attended: bfloat16 [384, 128, 1024], P('lon', 'lat')
Inputs may be any that keep to these rules, and one draw needn't show every extreme that they name: `query_local`: entries of the neighbourhood queries and keys. `key_local`: entries of the neighbourhood queries and keys.
All inputs are finite; a program needn't handle non-finite values.
Results may differ from a plain program's by a relative error of at most 0.015.
Values may be sent and summed in bfloat16 or wider, within the bound.
No kernel may reach another device: no remote copies, remote signals or barrier semaphores. Data moves between devices by JAX's collectives and lax.ppermute only.
A program may use at most 64 MiB of HBM per device.

v0:
```python
import math
import jax
import jax.numpy as jnp
from jax import lax
from jax.sharding import PartitionSpec as P

STEPS = 4


def extended(block, sides, width):
    for axis, dim in sides:
        count = lax.axis_size(axis)
        forward = [(i, i + 1) for i in range(count - 1)]
        forward.append((count - 1, 0))
        backward = [(target, source) for source, target in forward]
        low = lax.ppermute(
            lax.slice_in_dim(block, block.shape[dim] - width, None, axis=dim), axis, forward
        )
        high = lax.ppermute(lax.slice_in_dim(block, 0, width, axis=dim), axis, backward)
        block = jnp.concatenate([low, block, high], axis=dim)
    return block


def from_behind(x, axis, by):
    count = lax.axis_size(axis)
    return lax.ppermute(x, axis, [(i, (i + by) % count) for i in range(count)])


def offset_table(cells, span, window):
    query_pos = lax.broadcasted_iota(jnp.int32, (cells, span, window), 0)
    key_pos = lax.broadcasted_iota(jnp.int32, (cells, span, window), 1)
    offset = lax.broadcasted_iota(jnp.int32, (cells, span, window), 2)
    return (key_pos - query_pos == offset).astype(jnp.float32)


def fold_rows(left, weight_rows):
    return jnp.dot(left, weight_rows, preferred_element_type=jnp.float32)


def block_merge(carry_state, query_heads, key_block, score_scale):
    running_max, denominator, accumulated = carry_state
    head_count = query_heads.shape[1]
    head_size = query_heads.shape[2]
    keys_part = key_block[0].reshape(key_block.shape[1], head_count, head_size)
    values_part = key_block[1].reshape(key_block.shape[1], head_count, head_size)
    scores = (
        jnp.einsum("qhd,khd->hqk", query_heads, keys_part, preferred_element_type=jnp.float32)
        * score_scale
    )
    new_max = jnp.maximum(running_max, jnp.max(scores, axis=2))
    factor = jnp.exp(running_max - new_max)
    weights = jnp.exp(scores - new_max[:, :, None])
    denominator = denominator * factor + jnp.sum(weights, axis=2)
    weighted = jnp.einsum(
        "hqk,khd->hqd",
        weights.astype(jnp.bfloat16),
        values_part,
        preferred_element_type=jnp.float32,
    )
    accumulated = accumulated * factor[:, :, None] + weighted
    return (new_max, denominator, accumulated)


def body(
    tokens,
    query_local,
    key_local,
    value_local,
    position_bias,
    output_weight,
    norm_gain,
    global_weight,
):
    lon_cells, lat_cells, model_width = tokens.shape
    head_count = position_bias.shape[0]
    radius = (position_bias.shape[1] - 1) // 2
    window = 2 * radius + 1
    head_size = model_width // head_count
    score_scale = 1.0 / math.sqrt(head_size)
    token_count = lon_cells * lat_cells
    lon_span = lon_cells + 2 * radius
    lat_span = lat_cells + 2 * radius
    stacked = jnp.stack([key_local, value_local])
    padded = extended(stacked, (("lon", 1), ("lat", 2)), radius)
    window_keys = padded[0].reshape(lon_span * lat_span, head_count, head_size)
    window_values = padded[1].reshape(lon_span * lat_span, head_count, head_size)
    query_heads = query_local.reshape(token_count, head_count, head_size)
    lon_table = offset_table(lon_cells, lon_span, window)
    lat_table = offset_table(lat_cells, lat_span, window)
    lat_start = lax.axis_index("lat") * lat_cells
    lat_total = lat_cells * lax.axis_size("lat")
    lat_global = lat_start + jnp.arange(lat_span, dtype=jnp.int32) - radius
    lat_inside = (lat_global >= 0) & (lat_global < lat_total)
    lon_near = jnp.sum(lon_table, axis=2) > 0.5
    lat_near = (jnp.sum(lat_table, axis=2) > 0.5) & lat_inside[None, :]
    allowed = (lon_near[:, None, :, None] & lat_near[None, :, None, :]).reshape(
        token_count, lon_span * lat_span
    )

    def one_head(operands):
        query_one, key_one, value_one, bias_one = operands
        bias_lat = jnp.einsum("ab,jkb->ajk", bias_one, lat_table, precision=lax.Precision.HIGHEST)
        bias_full = jnp.einsum(
            "ajk,ila->ijlk", bias_lat, lon_table, precision=lax.Precision.HIGHEST
        )
        bias_full = bias_full.reshape(token_count, lon_span * lat_span)
        scores = jnp.einsum("qd,kd->qk", query_one, key_one, preferred_element_type=jnp.float32)
        scores = jnp.where(allowed, scores * score_scale + bias_full, -1e30)
        largest = jnp.max(scores, axis=1, keepdims=True)
        weights = jnp.exp(scores - largest)
        denominator = jnp.sum(weights, axis=1, keepdims=True)
        weighted = jnp.dot(
            weights.astype(jnp.bfloat16), value_one, preferred_element_type=jnp.float32
        )
        return (weighted / denominator).astype(jnp.bfloat16)

    head_outputs = lax.map(
        one_head,
        (
            jnp.transpose(query_heads, (1, 0, 2)),
            jnp.transpose(window_keys, (1, 0, 2)),
            jnp.transpose(window_values, (1, 0, 2)),
            position_bias,
        ),
    )
    local_out = jnp.transpose(head_outputs, (1, 0, 2)).reshape(token_count, model_width)
    flat_tokens = tokens.reshape(token_count, model_width)
    projected = fold_rows(local_out, lax.all_gather(output_weight, "lat", axis=0, tiled=True))
    hidden = (flat_tokens.astype(jnp.float32) + projected).astype(jnp.bfloat16)
    widened_hidden = hidden.astype(jnp.float32)
    inverse = lax.rsqrt(jnp.mean(widened_hidden * widened_hidden, axis=1, keepdims=True) + 1e-06)
    normed = (widened_hidden * inverse * norm_gain).astype(jnp.bfloat16)
    triple = fold_rows(normed, lax.all_gather(global_weight, "lat", axis=0, tiled=True))
    triple = triple.astype(jnp.bfloat16)
    global_query = triple[:, :model_width].reshape(token_count, head_count, head_size)
    key_pair = jnp.stack([triple[:, model_width : 2 * model_width], triple[:, 2 * model_width :]])
    carry_state = (
        jnp.full((head_count, token_count), -1e30, jnp.float32),
        jnp.zeros((head_count, token_count), jnp.float32),
        jnp.zeros((head_count, token_count, head_size), jnp.float32),
    )
    carry_state = block_merge(carry_state, global_query, key_pair, score_scale)
    travelling = key_pair
    for hop_index in range(STEPS):
        travelling = from_behind(travelling, ("lon", "lat"), 1)
        carry_state = block_merge(carry_state, global_query, travelling, score_scale)
    running_max, denominator, accumulated = carry_state
    attended = accumulated / denominator[:, :, None]
    attended = (
        jnp.transpose(attended, (1, 0, 2))
        .reshape(lon_cells, lat_cells, model_width)
        .astype(jnp.bfloat16)
    )
    return (hidden.reshape(lon_cells, lat_cells, model_width), attended)


def solution(mesh):
    return jax.shard_map(
        body,
        mesh=mesh,
        in_specs=(
            P("lon", "lat", None),
            P("lon", "lat", None),
            P("lon", "lat", None),
            P("lon", "lat", None),
            P(),
            P("lat", None),
            P(),
            P("lat", None),
        ),
        out_specs=(P("lon", "lat", None), P("lon", "lat", None)),
        check_vma=False,
    )
```

profile of v0, /device:TPU:313, one launch (start us, length us, event | category | flops | bytes accessed | tf_op | source)
XLA Modules:
  0.0 309.6 jit_solution(16309423687903335286)
XLA Ops:
  7.9 1.2 copy_bitcast_fusion.2
  9.3 2.9 collective-permute-start
  12.2 2.1 collective-permute-start.1
  14.3 1.2 collective-permute-done
  15.5 6.6 %collective-permute-done.1 = bf16[2,6,8,1024]{3,1,2,0:T(8,128)(2,1)S(1)} collective-permute-done((bf16[2,6,8,1024]{3,1,2,0:T(8,128)(2,1)S(1)}, bf16[2,6,8,1024]{3,1,2,0:T(8,128)(2,1)S(1)}, u32[]{:S(2)}, u32[]{:S(2)}) %collective-permute-start.1) | collective-permute-done | bytes 196640 | tf_op jit(solution)/shard_map/ppermute | solution.py:19
  23.5 3.1 %collective-permute-start.2 = (bf16[2,24,6,1024]{3,1,2,0:T(8,128)(2,1)}, bf16[2,24,6,1024]{3,1,2,0:T(8,128)(2,1)S(1)}, u32[]{:S(2)}, u32[]{:S(2)}) collective-permute-start(bf16[2,24,6,1024]{3,1,2,0:T(8,128)(2,1)} %get-tuple-element.126), channel_id=1, source_target_pairs={{0,1},{1,2},{2,3},{3,4},{4,5},{5,6},{6,7},{7,8},{8,9},{9,10},{10,1... | collective-permute-start | bytes 1769480 | tf_op jit(solution)/shard_map/ppermute | solution.py:16
  26.6 6.4 %collective-permute-start.3 = (bf16[2,24,6,1024]{3,1,2,0:T(8,128)(2,1)S(1)}, bf16[2,24,6,1024]{3,1,2,0:T(8,128)(2,1)}, u32[]{:S(2)}, u32[]{:S(2)}) collective-permute-start(bf16[2,24,6,1024]{3,1,2,0:T(8,128)(2,1)S(1)} %get-tuple-element.127), channel_id=1, source_target_pairs={{1,0},{2,1},{3,2},{4,3},{5,4},{6,5},{7,6},{8,7},{9,8},{10,9},{11,1... | collective-permute-start | bytes 1769480 | tf_op jit(solution)/shard_map/ppermute | solution.py:19
  33.6 26.1 %collective-permute-done.2 = bf16[2,24,6,1024]{3,1,2,0:T(8,128)(2,1)S(1)} collective-permute-done((bf16[2,24,6,1024]{3,1,2,0:T(8,128)(2,1)}, bf16[2,24,6,1024]{3,1,2,0:T(8,128)(2,1)S(1)}, u32[]{:S(2)}, u32[]{:S(2)}) %collective-permute-start.2) | collective-permute-done | bytes 589856 | tf_op jit(solution)/shard_map/ppermute | solution.py:16
  59.6 1.6 pad_maximum_fusion
  62.9 1.3 reshape_squeeze.30
  64.3 1.8 copy.86
  66.7 1.3 reshape_squeeze.31
  68.0 1.8 copy.88
  69.8 103.0 %while.11 = (s32[]{:T(128)}, bf16[16,96,64]{1,2,0:T(8,128)(2,1)S(1)}, bf16[16,96,64]{2,1,0:T(8,128)(2,1)S(1)}, bf16[16,480,64]{2,1,0:T(8,128)(2,1)}, f32[16,13,1...) while((s32[]{:T(128)}, ...), condition=%wide.region_5.6_spmd.clone, body=%wide.region_2.5_spmd.clone.sunk | while | flops 19753728 | bytes 2181005 | solution.py:117
  73.7 1.2 fusion.121
  144.5 1.2 fusion.121
  170.2 1.2 fusion.121
  172.8 2.3 fusion.48
  175.1 17.7 %all-gather.5.cloned.1.call-done = bf16[1024,3072]{1,0:T(8,128)(2,1)} async-done(((bf16[64,3072]{1,0:T(8,128)(2,1)}), bf16[1024,3072]{1,0:T(8,128)(2,1)}) %all-gather.5.cloned.1.call-update) | async-done | bytes 6291472 | tf_op jit(solution)/shard_map/all_gather | solution.py:133
  192.9 4.0 %convolution_convert_fusion = bf16[96,3072]{1,0:T(8,128)(2,1)S(1)} fusion(bf16[1024,3072]{1,0:T(8,128)(2,1)} %all-gather.5.cloned.1.call-done, bf16[96,1024]{1,0:T(8,128)(2,1)S(1)} %get-tuple-element.147, f32[1024]{0:T(1024)S(1)} %copy-done.10, f32[96]{0:T(128)S(1)} %add_rsqrt_fusion), kind=kOutput, calls=%fused_computation.32 | convolution fusion | flops 604667904 | bytes 7082368 | tf_op jit(solution)/shard_map/dot_general | solution.py:37
  197.0 3.2 %collective-permute-start.4 = (bf16[2,96,1024]{2,1,0:T(8,128)(2,1)S(1)}, bf16[2,96,1024]{2,1,0:T(8,128)(2,1)S(1)}, u32[]{:S(2)}, u32[]{:S(2)}) collective-permute-start(bf16[2,96,1024]{2,1,0:T(8,128)(2,1)S(1)} %pad_maximum_fusion.2), channel_id=1, source_target_pairs={{0,1},{1,2},{2,3},{3,4},{4,5},{5,6},{6,7},{7,8},{8,9},{9,10},{10,1... | collective-permute-start | bytes 1179656 | tf_op jit(solution)/shard_map/ppermute | solution.py:26
  201.8 20.7 %collective-permute-done.4 = bf16[2,96,1024]{2,1,0:T(8,128)(2,1)S(1)} collective-permute-done((bf16[2,96,1024]{2,1,0:T(8,128)(2,1)S(1)}, bf16[2,96,1024]{2,1,0:T(8,128)(2,1)S(1)}, u32[]{:S(2)}, u32[]{:S(2)}) %collective-permute-start.4) | collective-permute-done | bytes 393248 | tf_op jit(solution)/shard_map/ppermute | solution.py:26
  222.5 1.9 collective-permute-start.5
  225.8 22.2 %collective-permute-done.5 = bf16[2,96,1024]{2,1,0:T(8,128)(2,1)} collective-permute-done((bf16[2,96,1024]{2,1,0:T(8,128)(2,1)S(1)}, bf16[2,96,1024]{2,1,0:T(8,128)(2,1)}, u32[]{:S(2)}, u32[]{:S(2)}) %collective-permute-start.5) | collective-permute-done | bytes 393248 | tf_op jit(solution)/shard_map/ppermute | solution.py:26
  247.9 1.9 collective-permute-start.6
  252.3 17.8 %collective-permute-done.6 = bf16[2,96,1024]{2,1,0:T(8,128)(2,1)} collective-permute-done((bf16[2,96,1024]{2,1,0:T(8,128)(2,1)}, bf16[2,96,1024]{2,1,0:T(8,128)(2,1)}, u32[]{:S(2)}, u32[]{:S(2)}) %collective-permute-start.6) | collective-permute-done | bytes 393248 | tf_op jit(solution)/shard_map/ppermute | solution.py:26
  270.1 2.1 collective-permute-start.7
  274.9 1.3 fusion.85
  276.2 15.4 %collective-permute-done.7 = bf16[2,96,1024]{2,1,0:T(8,128)(2,1)} collective-permute-done((bf16[2,96,1024]{2,1,0:T(8,128)(2,1)}, bf16[2,96,1024]{2,1,0:T(8,128)(2,1)}, u32[]{:S(2)}, u32[]{:S(2)}) %collective-permute-start.7) | collective-permute-done | bytes 393248 | tf_op jit(solution)/shard_map/ppermute | solution.py:26
  291.6 1.8 fusion.80
  293.3 1.8 copy.102
  295.1 2.1 fusion.84
  (232 shorter events, 116.9 us)
Async XLA Ops:
  7.2 165.7 %all-gather.3.cloned.1.call-start = ((), (), s32[]{:S(2)}) async-start(), calls=%async_computation | async-start | bytes 2228224 | tf_op jit(solution)/shard_map/all_gather | solution.py:128
  7.9 185.0 %all-gather.5.cloned.1.call-start = ((), (), s32[]{:S(2)}) async-start(), calls=%async_computation.1 | async-start | bytes 6684672 | tf_op jit(solution)/shard_map/all_gather | solution.py:133
  9.3 6.2 %collective-permute-start = (bf16[2,6,8,1024]{3,1,2,0:T(8,128)(2,1)S(1)}, bf16[2,6,8,1024]{3,1,2,0:T(8,128)(2,1)S(1)}, u32[]{:S(2)}, u32[]{:S(2)}) collective-permute-start(bf16[2,6,8,1024]{3,1,2,0:T(8,128)(2,1)S(1)} %get-tuple-element.133), channel_id=1, source_target_pairs={{0,16},{16,32},{32,48},{48,64},{64,80},{80,96},{96,112},{112,128},... | collective-permute-start | bytes 589832 | tf_op jit(solution)/shard_map/ppermute | solution.py:16
  12.2 20.9 %copy-start.9 = (bf16[12,8,1024]{2,1,0:T(8,128)(2,1)S(1)}, bf16[12,8,1024]{2,1,0:T(8,128)(2,1)}, u32[]{:S(2)}) copy-start(bf16[12,8,1024]{2,1,0:T(8,128)(2,1)} %param.11) | copy-start | bytes 589828
  12.2 9.9 %collective-permute-start.1 = (bf16[2,6,8,1024]{3,1,2,0:T(8,128)(2,1)S(1)}, bf16[2,6,8,1024]{3,1,2,0:T(8,128)(2,1)S(1)}, u32[]{:S(2)}, u32[]{:S(2)}) collective-permute-start(bf16[2,6,8,1024]{3,1,2,0:T(8,128)(2,1)S(1)} %get-tuple-element.134), channel_id=1, source_target_pairs={{16,0},{32,16},{48,32},{64,48},{80,64},{96,80},{112,96},{128,112},... | collective-permute-start | bytes 589832 | tf_op jit(solution)/shard_map/ppermute | solution.py:19
  23.5 36.1 %collective-permute-start.2 = (bf16[2,24,6,1024]{3,1,2,0:T(8,128)(2,1)}, bf16[2,24,6,1024]{3,1,2,0:T(8,128)(2,1)S(1)}, u32[]{:S(2)}, u32[]{:S(2)}) collective-permute-start(bf16[2,24,6,1024]{3,1,2,0:T(8,128)(2,1)} %get-tuple-element.126), channel_id=1, source_target_pairs={{0,1},{1,2},{2,3},{3,4},{4,5},{5,6},{6,7},{7,8},{8,9},{9,10},{10,1... | collective-permute-start | bytes 1769480 | tf_op jit(solution)/shard_map/ppermute | solution.py:16
  26.6 33.0 %collective-permute-start.3 = (bf16[2,24,6,1024]{3,1,2,0:T(8,128)(2,1)S(1)}, bf16[2,24,6,1024]{3,1,2,0:T(8,128)(2,1)}, u32[]{:S(2)}, u32[]{:S(2)}) collective-permute-start(bf16[2,24,6,1024]{3,1,2,0:T(8,128)(2,1)S(1)} %get-tuple-element.127), channel_id=1, source_target_pairs={{1,0},{2,1},{3,2},{4,3},{5,4},{6,5},{7,6},{8,7},{9,8},{10,9},{11,1... | collective-permute-start | bytes 1769480 | tf_op jit(solution)/shard_map/ppermute | solution.py:19
  64.3 1.9 copy-start
  68.0 1.8 copy-start.7
  69.8 103.1 %copy-start.8 = (bf16[12,8,1024]{2,1,0:T(8,128)(2,1)S(1)}, bf16[12,8,1024]{2,1,0:T(8,128)(2,1)}, u32[]{:S(2)}) copy-start(bf16[12,8,1024]{2,1,0:T(8,128)(2,1)} %param.10) | copy-start | bytes 589828
  172.8 20.1 %copy-start.10 = (f32[1024]{0:T(1024)S(1)}, f32[1024]{0:T(1024)}, u32[]{:S(2)}) copy-start(f32[1024]{0:T(1024)} %param.16) | copy-start | bytes 12292
  175.1 21.7 %copy-start.6 = (bf16[96,1024]{1,0:T(8,128)(2,1)}, bf16[96,1024]{1,0:T(8,128)(2,1)S(1)}, u32[]{:S(2)}) copy-start(bf16[96,1024]{1,0:T(8,128)(2,1)S(1)} %get-tuple-element.147) | copy-start | bytes 589828
  197.0 25.4 %collective-permute-start.4 = (bf16[2,96,1024]{2,1,0:T(8,128)(2,1)S(1)}, bf16[2,96,1024]{2,1,0:T(8,128)(2,1)S(1)}, u32[]{:S(2)}, u32[]{:S(2)}) collective-permute-start(bf16[2,96,1024]{2,1,0:T(8,128)(2,1)S(1)} %pad_maximum_fusion.2), channel_id=1, source_target_pairs={{0,1},{1,2},{2,3},{3,4},{4,5},{5,6},{6,7},{7,8},{8,9},{9,10},{10,1... | collective-permute-start | bytes 1179656 | tf_op jit(solution)/shard_map/ppermute | solution.py:26
  222.5 25.5 %collective-permute-start.5 = (bf16[2,96,1024]{2,1,0:T(8,128)(2,1)S(1)}, bf16[2,96,1024]{2,1,0:T(8,128)(2,1)}, u32[]{:S(2)}, u32[]{:S(2)}) collective-permute-start(bf16[2,96,1024]{2,1,0:T(8,128)(2,1)S(1)} %collective-permute-done.4), channel_id=1, source_target_pairs={{0,1},{1,2},{2,3},{3,4},{4,5},{5,6},{6,7},{7,8},{8,9},{9,10},{10,1... | collective-permute-start | bytes 1179656 | tf_op jit(solution)/shard_map/ppermute | solution.py:26
  247.9 22.1 %collective-permute-start.6 = (bf16[2,96,1024]{2,1,0:T(8,128)(2,1)}, bf16[2,96,1024]{2,1,0:T(8,128)(2,1)}, u32[]{:S(2)}, u32[]{:S(2)}) collective-permute-start(bf16[2,96,1024]{2,1,0:T(8,128)(2,1)} %collective-permute-done.5), channel_id=1, source_target_pairs={{0,1},{1,2},{2,3},{3,4},{4,5},{5,6},{6,7},{7,8},{8,9},{9,10},{10,1... | collective-permute-start | bytes 1179656 | tf_op jit(solution)/shard_map/ppermute | solution.py:26
  270.1 21.5 %collective-permute-start.7 = (bf16[2,96,1024]{2,1,0:T(8,128)(2,1)}, bf16[2,96,1024]{2,1,0:T(8,128)(2,1)}, u32[]{:S(2)}, u32[]{:S(2)}) collective-permute-start(bf16[2,96,1024]{2,1,0:T(8,128)(2,1)} %collective-permute-done.6), channel_id=1, source_target_pairs={{0,1},{1,2},{2,3},{3,4},{4,5},{5,6},{6,7},{7,8},{8,9},{9,10},{10,1... | collective-permute-start | bytes 1179656 | tf_op jit(solution)/shard_map/ppermute | solution.py:26
  298.4 1.1 copy-start.1
  298.4 1.3 copy-start.2
  298.7 1.3 copy-start.3
  299.6 1.0 copy-start.4
  300.0 1.0 copy-start.5
Sparse Core Ops, SparseCore 0:
  11.0 77.9 all-gather.2
  92.0 100.8 all-gather.4
where the time goes:
time: 312 us; the launch traced here: 310 us
  waiting for transfers between devices  128 us (41%)
  matrix products  71.3 us (23%)
  local copies, waits for them, and re-layouts  61.4 us (20%)
  starting transfers between devices  23.6 us (8%)
  between operations  14.5 us (5%)
  other arithmetic  9.46 us (3%)
    ppermute x4, waiting for transfers between devices, from_behind(): return lax.ppermute(x, axis, [(i, (i + by) % count) for i in range(count)])  76 us
    ppermute x2, waiting for transfers between devices, extended(): lax.ppermute(lax.slice_in_dim(block, block.shape[dim] - width, None, axis...  27.3 us
    dot_general x16, matrix products, one_head(): jnp.einsum('qd,kd->qk', query_one, key_one, preferred_element_type=jnp.fl...  19.4 us
    dot_general x16, matrix products, one_head(): jnp.dot(weights.astype(jnp.bfloat16), value_one, preferred_element_type=j...  18.6 us
    dot_general x16, matrix products, one_head(): jnp.einsum('ajk,ila->ijlk', bias_lat, lon_table, precision=lax.Precision....  18.3 us
    all_gather x1, waiting for transfers between devices, body(): lax.all_gather(global_weight, 'lat', axis=0, tiled=True)  17.7 us
    dynamic_slice x16, local copies, waits for them, and re-layouts, body(): lax.map(one_head, (jnp.transpose(query_heads, (1, 0, 2)), jnp.transpose(w...  13.2 us
    transpose x16, local copies, waits for them, and re-layouts, one_head(): jnp.einsum('ajk,ila->ijlk', bias_lat, lon_table, precision=lax.Precision....  10.1 us
  transfers between devices with their start and end apart: 10, of which 8 were waited for; matrix products, arithmetic and copies ran while one was open for 41% of the time, Pallas kernels for 0%

commit v1 on v0

--- a/solution.py
+++ b/solution.py
@@ -130,7 +130,12 @@
     widened_hidden = hidden.astype(jnp.float32)
     inverse = lax.rsqrt(jnp.mean(widened_hidden * widened_hidden, axis=1, keepdims=True) + 1e-06)
     normed = (widened_hidden * inverse * norm_gain).astype(jnp.bfloat16)
-    triple = fold_rows(normed, lax.all_gather(global_weight, "lat", axis=0, tiled=True))
+    triple = fold_rows(
+        normed,
+        jnp.concatenate(
+            lax.all_to_all(jnp.stack([global_weight] * lax.axis_size("lat")), "lat", 0, 0), axis=0
+        ),
+    )
     triple = triple.astype(jnp.bfloat16)
     global_query = triple[:, :model_width].reshape(token_count, head_count, head_size)
     key_pair = jnp.stack([triple[:, model_width : 2 * model_width], triple[:, 2 * model_width :]])

time: 312 us -> 348 us (1.12)
  the two profiles are of different devices: /device:TPU:313 before, /device:TPU:57 now
where the time goes in v1:
time: 348 us; the launch traced here: 346 us
  waiting for transfers between devices  153 us (44%)
  matrix products  70.5 us (20%)
  local copies, waits for them, and re-layouts  65.4 us (19%)
  starting transfers between devices  32.6 us (9%)
  between operations  14.5 us (4%)
  other arithmetic  9.44 us (3%)
    ppermute x4, waiting for transfers between devices, from_behind(): return lax.ppermute(x, axis, [(i, (i + by) % count) for i in range(count)])  82.2 us
    all_gather x1, waiting for transfers between devices, body(): lax.all_gather(output_weight, 'lat', axis=0, tiled=True)  41.2 us
    ppermute x2, waiting for transfers between devices, extended(): lax.ppermute(lax.slice_in_dim(block, 0, width, axis=dim), axis, backward)  27.3 us
    dot_general x16, matrix products, one_head(): jnp.einsum('qd,kd->qk', query_one, key_one, preferred_element_type=jnp.fl...  19.4 us
    dot_general x16, matrix products, one_head(): jnp.dot(weights.astype(jnp.bfloat16), value_one, preferred_element_type=j...  18.6 us
    dot_general x16, matrix products, one_head(): jnp.einsum('ajk,ila->ijlk', bias_lat, lon_table, precision=lax.Precision....  18.3 us
    dynamic_slice x16, local copies, waits for them, and re-layouts, body(): lax.map(one_head, (jnp.transpose(query_heads, (1, 0, 2)), jnp.transpose(w...  13.2 us
    ppermute x2, starting transfers between devices, extended(): lax.ppermute(lax.slice_in_dim(block, 0, width, axis=dim), axis, backward)  12.8 us
  transfers between devices with their start and end apart: 10, of which 9 were waited for; matrix products, arithmetic and copies ran while one was open for 37% of the time, Pallas kernels for 0%

profile of v1, /device:TPU:57, one launch (start us, length us, event | category | flops | bytes accessed | tf_op | source)
XLA Modules:
  0.0 345.9 jit_solution(15131721615536444638)
XLA Ops:
  7.2 1.2 copy_bitcast_fusion.2
  8.6 3.8 %collective-permute-start = (bf16[2,6,8,1024]{3,1,2,0:T(8,128)(2,1)S(1)}, bf16[2,6,8,1024]{3,1,2,0:T(8,128)(2,1)S(1)}, u32[]{:S(2)}, u32[]{:S(2)}) collective-permute-start(bf16[2,6,8,1024]{3,1,2,0:T(8,128)(2,1)S(1)} %get-tuple-element.133), channel_id=1, source_target_pairs={{0,16},{16,32},{32,48},{48,64},{64,80},{80,96},{96,112},{112,128},... | collective-permute-start | bytes 589832 | tf_op jit(solution)/shard_map/ppermute | solution.py:16
  12.4 2.1 collective-permute-start.1
  15.6 6.6 %collective-permute-done.1 = bf16[2,6,8,1024]{3,1,2,0:T(8,128)(2,1)S(1)} collective-permute-done((bf16[2,6,8,1024]{3,1,2,0:T(8,128)(2,1)S(1)}, bf16[2,6,8,1024]{3,1,2,0:T(8,128)(2,1)S(1)}, u32[]{:S(2)}, u32[]{:S(2)}) %collective-permute-start.1) | collective-permute-done | bytes 196640 | tf_op jit(solution)/shard_map/ppermute | solution.py:19
  23.6 3.1 collective-permute-start.2
  26.8 10.8 %collective-permute-start.3 = (bf16[2,24,6,1024]{3,1,2,0:T(8,128)(2,1)S(1)}, bf16[2,24,6,1024]{3,1,2,0:T(8,128)(2,1)}, u32[]{:S(2)}, u32[]{:S(2)}) collective-permute-start(bf16[2,24,6,1024]{3,1,2,0:T(8,128)(2,1)S(1)} %get-tuple-element.127), channel_id=1, source_target_pairs={{1,0},{2,1},{3,2},{4,3},{5,4},{6,5},{7,6},{8,7},{9,8},{10,9},{11,1... | collective-permute-start | bytes 1769480 | tf_op jit(solution)/shard_map/ppermute | solution.py:19
  37.6 3.4 stack.17
  41.0 5.0 %all-to-all-start = ((bf16[16,64,3072]{2,1,0:T(8,128)(2,1)}), bf16[16,64,3072]{2,1,0:T(8,128)(2,1)}, u32[]{:S(2)}, u32[]{:S(2)}) async-start(bf16[16,64,3072]{2,1,0:T(8,128)(2,1)} %stack.17), calls=%async_computation | async-start | bytes 12582912 | tf_op jit(solution)/shard_map/all_to_all | solution.py:136
  47.2 20.6 %collective-permute-done.3 = bf16[2,24,6,1024]{3,1,2,0:T(8,128)(2,1)} collective-permute-done((bf16[2,24,6,1024]{3,1,2,0:T(8,128)(2,1)S(1)}, bf16[2,24,6,1024]{3,1,2,0:T(8,128)(2,1)}, u32[]{:S(2)}, u32[]{:S(2)}) %collective-permute-start.3) | collective-permute-done | bytes 589856 | tf_op jit(solution)/shard_map/ppermute | solution.py:19
  67.9 1.6 pad_maximum_fusion
  71.2 1.3 reshape_squeeze.31
  72.5 1.8 copy.88
  74.8 1.3 reshape_squeeze.30
  76.2 1.8 copy.86
  78.0 103.0 %while.11 = (s32[]{:T(128)}, bf16[16,96,64]{1,2,0:T(8,128)(2,1)S(1)}, bf16[16,96,64]{2,1,0:T(8,128)(2,1)S(1)}, bf16[16,480,64]{2,1,0:T(8,128)(2,1)}, f32[16,13,1...) while((s32[]{:T(128)}, ...), condition=%wide.region_5.6_spmd.clone, body=%wide.region_2.5_spmd.clone.sunk | while | flops 19753728 | bytes 2181013 | solution.py:117
  88.3 1.2 fusion.121
  181.0 41.2 %all-gather.2.cloned.1.call-done = bf16[1024,1024]{1,0:T(8,128)(2,1)} async-done(((bf16[64,1024]{1,0:T(8,128)(2,1)}), bf16[1024,1024]{1,0:T(8,128)(2,1)}) %all-gather.2.cloned.1.call-update) | async-done | bytes 2097168 | tf_op jit(solution)/shard_map/all_gather | solution.py:128
  222.3 2.2 fusion.48
  224.5 4.0 %convolution_convert_fusion = bf16[96,3072]{1,0:T(8,128)(2,1)S(1)} fusion(bf16[1024,3072]{1,0:T(8,128)(2,1)} %bitcast.9, bf16[96,1024]{1,0:T(8,128)(2,1)S(1)} %get-tuple-element.147, f32[1024]{0:T(1024)S(1)} %copy-done.11, f32[96]{0:T(128)S(1)} %add_rsqrt_fusion), kind=kOutput, calls=%fused_computation.32 | convolution fusion | flops 604667904 | bytes 7082368 | tf_op jit(solution)/shard_map/dot_general | solution.py:37
  228.7 1.9 collective-permute-start.4
  232.2 22.2 %collective-permute-done.4 = bf16[2,96,1024]{2,1,0:T(8,128)(2,1)S(1)} collective-permute-done((bf16[2,96,1024]{2,1,0:T(8,128)(2,1)S(1)}, bf16[2,96,1024]{2,1,0:T(8,128)(2,1)S(1)}, u32[]{:S(2)}, u32[]{:S(2)}) %collective-permute-start.4) | collective-permute-done | bytes 393248 | tf_op jit(solution)/shard_map/ppermute | solution.py:26
  254.4 1.9 collective-permute-start.5
  257.7 27.1 %collective-permute-done.5 = bf16[2,96,1024]{2,1,0:T(8,128)(2,1)} collective-permute-done((bf16[2,96,1024]{2,1,0:T(8,128)(2,1)S(1)}, bf16[2,96,1024]{2,1,0:T(8,128)(2,1)}, u32[]{:S(2)}, u32[]{:S(2)}) %collective-permute-start.5) | collective-permute-done | bytes 393248 | tf_op jit(solution)/shard_map/ppermute | solution.py:26
  284.8 2.1 collective-permute-start.6
  289.3 16.8 %collective-permute-done.6 = bf16[2,96,1024]{2,1,0:T(8,128)(2,1)} collective-permute-done((bf16[2,96,1024]{2,1,0:T(8,128)(2,1)}, bf16[2,96,1024]{2,1,0:T(8,128)(2,1)}, u32[]{:S(2)}, u32[]{:S(2)}) %collective-permute-start.6) | collective-permute-done | bytes 393248 | tf_op jit(solution)/shard_map/ppermute | solution.py:26
  306.1 1.9 collective-permute-start.7
  310.8 1.3 fusion.85
  312.1 16.0 %collective-permute-done.7 = bf16[2,96,1024]{2,1,0:T(8,128)(2,1)} collective-permute-done((bf16[2,96,1024]{2,1,0:T(8,128)(2,1)}, bf16[2,96,1024]{2,1,0:T(8,128)(2,1)}, u32[]{:S(2)}, u32[]{:S(2)}) %collective-permute-start.7) | collective-permute-done | bytes 393248 | tf_op jit(solution)/shard_map/ppermute | solution.py:26
  328.1 1.8 fusion.80
  329.9 1.8 copy.103
  331.6 1.8 copy.102
  333.4 1.3 fusion.84
  (234 shorter events, 119.4 us)
Async XLA Ops:
  7.2 215.1 %all-gather.2.cloned.1.call-start = ((), (), s32[]{:S(2)}) async-start(), calls=%async_computation.1 | async-start | bytes 2228224 | tf_op jit(solution)/shard_map/all_gather | solution.py:128
  8.6 7.1 %collective-permute-start = (bf16[2,6,8,1024]{3,1,2,0:T(8,128)(2,1)S(1)}, bf16[2,6,8,1024]{3,1,2,0:T(8,128)(2,1)S(1)}, u32[]{:S(2)}, u32[]{:S(2)}) collective-permute-start(bf16[2,6,8,1024]{3,1,2,0:T(8,128)(2,1)S(1)} %get-tuple-element.133), channel_id=1, source_target_pairs={{0,16},{16,32},{32,48},{48,64},{64,80},{80,96},{96,112},{112,128},... | collective-permute-start | bytes 589832 | tf_op jit(solution)/shard_map/ppermute | solution.py:16
  12.3 25.2 %copy-start.6 = (bf16[64,3072]{1,0:T(8,128)(2,1)S(1)}, bf16[64,3072]{1,0:T(8,128)(2,1)}, u32[]{:S(2)}) copy-start(bf16[64,3072]{1,0:T(8,128)(2,1)} %param.17) | copy-start | bytes 1179652
  12.4 9.9 %collective-permute-start.1 = (bf16[2,6,8,1024]{3,1,2,0:T(8,128)(2,1)S(1)}, bf16[2,6,8,1024]{3,1,2,0:T(8,128)(2,1)S(1)}, u32[]{:S(2)}, u32[]{:S(2)}) collective-permute-start(bf16[2,6,8,1024]{3,1,2,0:T(8,128)(2,1)S(1)} %get-tuple-element.134), channel_id=1, source_target_pairs={{16,0},{32,16},{48,32},{64,48},{80,64},{96,80},{112,96},{128,112},... | collective-permute-start | bytes 589832 | tf_op jit(solution)/shard_map/ppermute | solution.py:19
  23.6 23.6 %collective-permute-start.2 = (bf16[2,24,6,1024]{3,1,2,0:T(8,128)(2,1)}, bf16[2,24,6,1024]{3,1,2,0:T(8,128)(2,1)S(1)}, u32[]{:S(2)}, u32[]{:S(2)}) collective-permute-start(bf16[2,24,6,1024]{3,1,2,0:T(8,128)(2,1)} %get-tuple-element.126), channel_id=1, source_target_pairs={{0,1},{1,2},{2,3},{3,4},{4,5},{5,6},{6,7},{7,8},{8,9},{9,10},{10,1... | collective-permute-start | bytes 1769480 | tf_op jit(solution)/shard_map/ppermute | solution.py:16
  26.8 41.1 %collective-permute-start.3 = (bf16[2,24,6,1024]{3,1,2,0:T(8,128)(2,1)S(1)}, bf16[2,24,6,1024]{3,1,2,0:T(8,128)(2,1)}, u32[]{:S(2)}, u32[]{:S(2)}) collective-permute-start(bf16[2,24,6,1024]{3,1,2,0:T(8,128)(2,1)S(1)} %get-tuple-element.127), channel_id=1, source_target_pairs={{1,0},{2,1},{3,2},{4,3},{5,4},{6,5},{7,6},{8,7},{9,8},{10,9},{11,1... | collective-permute-start | bytes 1769480 | tf_op jit(solution)/shard_map/ppermute | solution.py:19
  41.0 5.0 %copy-start.10 = (bf16[12,8,1024]{2,1,0:T(8,128)(2,1)S(1)}, bf16[12,8,1024]{2,1,0:T(8,128)(2,1)}, u32[]{:S(2)}) copy-start(bf16[12,8,1024]{2,1,0:T(8,128)(2,1)} %param.11) | copy-start | bytes 589828
  41.0 183.5 %all-to-all-start = ((bf16[16,64,3072]{2,1,0:T(8,128)(2,1)}), bf16[16,64,3072]{2,1,0:T(8,128)(2,1)}, u32[]{:S(2)}, u32[]{:S(2)}) async-start(bf16[16,64,3072]{2,1,0:T(8,128)(2,1)} %stack.17), calls=%async_computation | async-start | bytes 12582912 | tf_op jit(solution)/shard_map/all_to_all | solution.py:136
  72.5 1.8 copy-start
  76.2 1.8 copy-start.7
  78.0 144.3 %copy-start.9 = (bf16[12,8,1024]{2,1,0:T(8,128)(2,1)S(1)}, bf16[12,8,1024]{2,1,0:T(8,128)(2,1)}, u32[]{:S(2)}) copy-start(bf16[12,8,1024]{2,1,0:T(8,128)(2,1)} %param.10) | copy-start | bytes 589828
  181.0 43.5 %copy-start.11 = (f32[1024]{0:T(1024)S(1)}, f32[1024]{0:T(1024)}, u32[]{:S(2)}) copy-start(f32[1024]{0:T(1024)} %param.16) | copy-start | bytes 12292
  224.5 4.1 %copy-start.5 = (bf16[96,1024]{1,0:T(8,128)(2,1)}, bf16[96,1024]{1,0:T(8,128)(2,1)S(1)}, u32[]{:S(2)}) copy-start(bf16[96,1024]{1,0:T(8,128)(2,1)S(1)} %get-tuple-element.147) | copy-start | bytes 589828
  228.7 25.7 %collective-permute-start.4 = (bf16[2,96,1024]{2,1,0:T(8,128)(2,1)S(1)}, bf16[2,96,1024]{2,1,0:T(8,128)(2,1)S(1)}, u32[]{:S(2)}, u32[]{:S(2)}) collective-permute-start(bf16[2,96,1024]{2,1,0:T(8,128)(2,1)S(1)} %pad_maximum_fusion.2), channel_id=1, source_target_pairs={{0,1},{1,2},{2,3},{3,4},{4,5},{5,6},{6,7},{7,8},{8,9},{9,10},{10,1... | collective-permute-start | bytes 1179656 | tf_op jit(solution)/shard_map/ppermute | solution.py:26
  254.4 30.4 %collective-permute-start.5 = (bf16[2,96,1024]{2,1,0:T(8,128)(2,1)S(1)}, bf16[2,96,1024]{2,1,0:T(8,128)(2,1)}, u32[]{:S(2)}, u32[]{:S(2)}) collective-permute-start(bf16[2,96,1024]{2,1,0:T(8,128)(2,1)S(1)} %collective-permute-done.4), channel_id=1, source_target_pairs={{0,1},{1,2},{2,3},{3,4},{4,5},{5,6},{6,7},{7,8},{8,9},{9,10},{10,1... | collective-permute-start | bytes 1179656 | tf_op jit(solution)/shard_map/ppermute | solution.py:26
  284.8 21.3 %collective-permute-start.6 = (bf16[2,96,1024]{2,1,0:T(8,128)(2,1)}, bf16[2,96,1024]{2,1,0:T(8,128)(2,1)}, u32[]{:S(2)}, u32[]{:S(2)}) collective-permute-start(bf16[2,96,1024]{2,1,0:T(8,128)(2,1)} %collective-permute-done.5), channel_id=1, source_target_pairs={{0,1},{1,2},{2,3},{3,4},{4,5},{5,6},{6,7},{7,8},{8,9},{9,10},{10,1... | collective-permute-start | bytes 1179656 | tf_op jit(solution)/shard_map/ppermute | solution.py:26
  306.1 21.9 %collective-permute-start.7 = (bf16[2,96,1024]{2,1,0:T(8,128)(2,1)}, bf16[2,96,1024]{2,1,0:T(8,128)(2,1)}, u32[]{:S(2)}, u32[]{:S(2)}) collective-permute-start(bf16[2,96,1024]{2,1,0:T(8,128)(2,1)} %collective-permute-done.6), channel_id=1, source_target_pairs={{0,1},{1,2},{2,3},{3,4},{4,5},{5,6},{6,7},{7,8},{8,9},{9,10},{10,1... | collective-permute-start | bytes 1179656 | tf_op jit(solution)/shard_map/ppermute | solution.py:26
  334.7 1.0 copy-start.1
  335.0 1.0 copy-start.2
  335.5 1.0 copy-start.3
  336.0 1.0 copy-start.4
  336.5 1.0 copy-start.8
Sparse Core Ops, SparseCore 0:
  37.7 184.5 all-gather.1
